TPU v7x, 32 devices: a whole 2x2x4 slice. The times are simulated.
32 devices in a mesh: field: 2 (over x), focus: 2 (over core), strip: 8 (over z, y).
Axes of the slice: x: 2, y: 2, z: 4, core: 2. Of those that a mesh axis runs over, the one named last changes fastest.
Arguments:
- slices: bfloat16 [32, 4096, 4096], P(('field', 'focus'), 'strip'), parts along dimension 0, may hold values from 0 to 1
- otf_rows: float32 [4096], replicated, may hold values from 0.1 to 1
- otf_cols: float32 [4096], replicated, may hold values from 0.1 to 1
Outputs:
- restored: float32 [8192, 4096], P(('field', 'focus', 'strip')), parts along dimension 0
There are 2 independent parts, one for each index of `field`. A program takes and returns all parts, laid end to end along the dimension named above; an argument that names none is the same for every part. Nothing has to cross between parts.
All inputs are finite; a program needn't handle non-finite values.
Results may differ from a plain program's by a relative error of at most 0.011.
Values may be sent and summed in bfloat16 or wider, within the bound.
A program may use at most 256 MiB of HBM per device.

v0:
```python
import math

import jax
import jax.numpy as jnp
from jax import lax
from jax.sharding import PartitionSpec as P

floor_weight = 0.01
noise_ratio = 0.01


def extended(cells, sides, width):
    for axis, dim in sides:
        count = lax.axis_size(axis)
        ends = count - 1
        head = lax.slice_in_dim(cells, 0, width, axis=dim)
        tail = lax.slice_in_dim(cells, cells.shape[dim] - width, cells.shape[dim], axis=dim)
        cells = jnp.concatenate(
            [
                lax.ppermute(tail, axis, [(i, (i + 1) % count) for i in range(ends)]),
                cells,
                lax.ppermute(head, axis, [((i + 1) % count, i) for i in range(ends)]),
            ],
            axis=dim,
        )
    return cells


def cosine_block(first_row, height, length):
    low_count = min(64, length)
    high_count = length // low_count
    frequency = first_row + lax.broadcasted_iota(jnp.int32, (height, 1), 0)
    high_sample = lax.broadcasted_iota(jnp.int32, (1, high_count), 1)
    low_sample = lax.broadcasted_iota(jnp.int32, (1, low_count), 1)
    high_phase = 2 * low_count * high_sample * frequency % (4 * length)
    low_phase = (2 * low_sample + 1) * frequency % (4 * length)
    unit = jnp.float32(math.pi / (2 * length))
    high_angle = high_phase.astype(jnp.float32) * unit
    low_angle = low_phase.astype(jnp.float32) * unit
    norming = jnp.where(
        frequency == 0, jnp.float32(math.sqrt(1.0 / length)), jnp.float32(math.sqrt(2.0 / length))
    )
    high_cos = (norming * jnp.cos(high_angle))[:, :, None]
    high_sin = (norming * jnp.sin(high_angle))[:, :, None]
    low_cos = jnp.cos(low_angle)[:, None, :]
    low_sin = jnp.sin(low_angle)[:, None, :]
    table = high_cos * low_cos - high_sin * low_sin
    return table.reshape(height, length).astype(jnp.bfloat16)


def cosine_table(length):
    height = min(512, length)
    starts = jnp.arange(length // height, dtype=jnp.int32) * height
    return lax.map(lambda first_row: cosine_block(first_row, height, length), starts).reshape(
        length, length
    )


def laplace(padded, center, spacing, margin):
    count = center.shape[1]
    total = (
        padded[:, margin + spacing : margin + spacing + count, :]
        + padded[:, margin - spacing : margin - spacing + count, :]
    )
    widened = jnp.pad(center, ((0, 0), (0, 0), (spacing, spacing)))
    total = total + widened[:, :, 2 * spacing :] + widened[:, :, : -2 * spacing]
    return total - 4.0 * center


def contract(left, right, left_dim, right_dim):
    return lax.dot_general(
        left, right, (((left_dim,), (right_dim,)), ((), ())), preferred_element_type=jnp.float32
    )


def body(slices, otf_rows, otf_cols):
    focus_count = lax.axis_size("focus")
    strip_count = lax.axis_size("strip")
    length = slices.shape[2]
    piece = length // (focus_count * strip_count)
    margin = 4
    padded = extended(slices, (("strip", 1),), margin).astype(jnp.float32)
    center = padded[:, margin:-margin, :]
    fine_term = laplace(padded, center, 1, margin)
    middle_term = laplace(padded, center, 2, margin)
    coarse_term = laplace(padded, center, 4, margin)
    weight = (
        floor_weight
        + fine_term * fine_term
        + 0.5 * middle_term * middle_term
        + 0.25 * coarse_term * coarse_term
    )
    numerator = jnp.sum(weight * center, axis=0)
    denominator = jnp.sum(weight, axis=0)
    numerator, denominator = (
        lax.psum_scatter(numerator, "focus", scatter_dimension=0, tiled=True),
        lax.psum_scatter(denominator, "focus", scatter_dimension=0, tiled=True),
    )
    row_block = (numerator / denominator).astype(jnp.bfloat16)
    cosines = cosine_table(length)
    along_cols = contract(cosines, row_block, 1, 1).astype(jnp.bfloat16)
    arrived = lax.all_to_all(
        along_cols, ("focus", "strip"), split_axis=0, concat_axis=1, tiled=True
    )
    column_block = (
        arrived.reshape(piece, focus_count, strip_count, piece)
        .transpose(0, 2, 1, 3)
        .reshape(piece, length)
    )
    spectrum = contract(column_block, cosines, 1, 1)
    owner = lax.axis_index("focus") * strip_count + lax.axis_index("strip")
    local_cols = lax.dynamic_slice_in_dim(otf_cols, owner * piece, piece, 0)
    response = local_cols[:, None] * otf_rows[None, :]
    filtered = (spectrum * (response / (response * response + noise_ratio))).astype(jnp.bfloat16)
    back_cols = contract(cosines, filtered, 0, 1).astype(jnp.bfloat16)
    rows_back = lax.all_to_all(
        back_cols, ("focus", "strip"), split_axis=0, concat_axis=1, tiled=True
    )
    return jnp.dot(rows_back, cosines, preferred_element_type=jnp.float32)


def solution(mesh):
    in_specs = (P(("field", "focus"), "strip", None), P(), P())
    out_specs = P(("field", "focus", "strip"), None)
    return jax.shard_map(body, mesh=mesh, in_specs=in_specs, out_specs=out_specs, check_vma=False)
```

profile of v0, /device:TPU:0, one launch (start us, length us, event | category | flops | bytes accessed | tf_op | source)
XLA Modules:
  0.0 783.5 jit_solution(7468507866088875308)
XLA Ops:
  8.0 4.9 collective-permute-start
  14.2 9.8 %collective-permute-done = bf16[8,4,4096]{2,1,0:T(4,128)(2,1)S(1)} collective-permute-done((bf16[8,4,4096]{2,1,0:T(4,128)(2,1)S(1)}, bf16[8,4,4096]{2,1,0:T(4,128)(2,1)S(1)}, u32[]{:S(2)}, u32[]{:S(2)}) %collective-permute-start) | collective-permute-done | bytes 262176 | tf_op jit(solution)/shard_map/ppermute | solution.py:20
  24.1 32.4 %maximum_convert_fusion = f32[8,520,4096]{2,1,0:T(8,128)} fusion(bf16[8,4,4096]{2,1,0:T(4,128)(2,1)S(1)} %collective-permute-done.1, bf16[8,512,4096]{2,1,0:T(8,128)(2,1)} %param.5, bf16[8,4,4096]{2,1,0:T(4,128)(2,1)S(1)} %collective-permute-done), kind=kLoop, calls=%fused_computation.45 | loop fusion | flops 102236160 | bytes 102236160 | tf_op jit(solution)/shard_map/convert_element_type | solution.py:82
  56.4 44.1 %slice.62 = f32[8,512,4096]{2,1,0:T(8,128)} slice(f32[8,520,4096]{2,1,0:T(8,128)} %maximum_convert_fusion), slice={[0:8], [4:516], [0:4096]} | slice | bytes 134217728 | tf_op jit(solution)/shard_map/slice | solution.py:83
  100.5 343.3 %fusion.23 = (f32[512,4096]{1,0:T(8,128)}, f32[512,4096]{1,0:T(8,128)}) fusion(f32[8,520,4096]{2,1,0:T(8,128)} %maximum_convert_fusion, f32[8,512,4096]{2,1,0:T(8,128)} %slice.62), kind=kLoop, calls=%fused_computation.55 | loop fusion | flops 398458880 | bytes 553648128 | tf_op jit(solution)/shard_map/reduce_sum | solution.py:94
  444.6 145.0 %while.12 = (s32[]{:T(128)}, bf16[8,512,4096]{2,1,0:T(8,128)(2,1)}, s32[8]{0:T(128)S(1)}, s32[]{:T(128)}) while((s32[]{:T(128)}, bf16[8,512,4096]{2,1,0:T(8,128)(2,1)}, s32[8]{0:T(128)S(1)}, s32[]{:T(128)}) %tuple.37), condition=%wide.region_1.2_spmd, body=%wide.region_0.1_spmd.sunk | while | flops 9373890 | bytes 22029896 | solution.py:54
  451.4 6.9 copy.17
  458.3 5.6 constant_dynamic-update-slice_fusion.2
  470.7 6.6 copy.17
  477.4 5.5 constant_dynamic-update-slice_fusion.2
  489.7 6.4 copy.17
  507.5 6.4 copy.17
  525.3 6.4 copy.17
  543.1 6.4 copy.17
  549.4 4.6 constant_dynamic-update-slice_fusion.2
  560.9 6.4 copy.17
  567.2 4.6 constant_dynamic-update-slice_fusion.2
  578.6 6.4 copy.17
  589.7 18.7 %convolution_convert_fusion = bf16[4096,256]{1,0:T(8,128)(2,1)} fusion(bf16[4096,4096]{1,0:T(8,128)(2,1)} %bitcast.33, f32[256,4096]{1,0:T(8,128)} %reduce-scatter.3.cloned.1.call-done, f32[256,4096]{1,0:T(8,128)} %reduce-scatter.5.cloned.1.call-done), kind=kOutput, calls=%fused_computation.49 | convolution fusion | flops 8593080320 | bytes 44040192 | tf_op jit(solution)/shard_map/dot_general | solution.py:71
  608.4 6.3 all-to-all-start
  615.4 46.8 %all-to-all-done = bf16[16,256,256]{2,1,0:T(8,128)(2,1)S(1)} async-done(((bf16[16,256,256]{2,1,0:T(8,128)(2,1)}), bf16[16,256,256]{2,1,0:T(8,128)(2,1)S(1)}, u32[]{:S(2)}, u32[]{:S(2)}) %all-to-all-start) | async-done | bytes 2097184 | tf_op jit(solution)/shard_map/all_to_all | solution.py:102
  664.6 37.6 %convolution_convert_fusion.1 = bf16[4096,256]{1,0:T(8,128)(2,1)} fusion(bf16[4096,4096]{1,0:T(8,128)(2,1)} %bitcast.34, bf16[256,4096]{0,1:T(8,128)(2,1)} %bitcast.39, f32[4096]{0:T(1024)S(1)} %copy-done, f32[256]{0:T(256)S(1)} %dynamic_slice.10), kind=kOutput, calls=%fused_computation.51 | convolution fusion | flops 17187209216 | bytes 37766144 | tf_op jit(solution)/shard_map/dot_general | solution.py:71
  705.0 54.4 %all_to_all.35 = bf16[16,256,256]{1,2,0:T(8,128)(2,1)S(1)} all-to-all(bf16[16,256,256]{1,2,0:T(8,128)(2,1)S(1)} %copy.12), channel_id=1, replica_groups=mesh['field'=2,'focus'=2,'strip'=8] {'focus','strip'}, dimensions={0} | all-to-all | bytes 4194304 | tf_op jit(solution)/shard_map/all_to_all | solution.py:116
  759.5 17.2 %fusion.25 = f32[256,4096]{1,0:T(8,128)} fusion(bf16[256,4096]{0,1:T(8,128)(2,1)S(1)} %bitcast.36, bf16[4096,4096]{1,0:T(8,128)(2,1)} %bitcast.35), kind=kOutput, calls=%fused_computation.57 | convolution fusion | flops 8589934592 | bytes 39845888 | tf_op jit(solution)/shard_map/dot_general | solution.py:119
  (68 shorter events, 82.0 us)
Async XLA Ops:
  6.5 583.1 %reduce-scatter.3.cloned.1.call-start = ((), (), s32[]{:S(2)}) async-start(), calls=%async_computation.4 | async-start | bytes 12582912 | tf_op jit(solution)/shard_map/reduce_scatter | solution.py:96
  8.0 16.0 %collective-permute-start = (bf16[8,4,4096]{2,1,0:T(4,128)(2,1)S(1)}, bf16[8,4,4096]{2,1,0:T(4,128)(2,1)S(1)}, u32[]{:S(2)}, u32[]{:S(2)}) collective-permute-start(bf16[8,4,4096]{2,1,0:T(4,128)(2,1)S(1)} %get-tuple-element.64), channel_id=1, source_target_pairs={{0,1},{1,2},{2,3},{3,4},{4,5},{5,6},{6,7},{8,9},{9,10},{10,11},{11... | collective-permute-start | bytes 786440 | tf_op jit(solution)/shard_map/ppermute | solution.py:20
  12.9 11.2 %collective-permute-start.1 = (bf16[8,4,4096]{2,1,0:T(4,128)(2,1)S(1)}, bf16[8,4,4096]{2,1,0:T(4,128)(2,1)S(1)}, u32[]{:S(2)}, u32[]{:S(2)}) collective-permute-start(bf16[8,4,4096]{2,1,0:T(4,128)(2,1)S(1)} %get-tuple-element.65), channel_id=1, source_target_pairs={{1,0},{2,1},{3,2},{4,3},{5,4},{6,5},{7,6},{9,8},{10,9},{11,10},{12... | collective-permute-start | bytes 786440 | tf_op jit(solution)/shard_map/ppermute | solution.py:22
  443.9 145.8 %reduce-scatter.5.cloned.1.call-start = ((), (), s32[]{:S(2)}) async-start(), calls=%async_computation.5 | async-start | bytes 12582912 | tf_op jit(solution)/shard_map/reduce_scatter | solution.py:97
  589.7 74.9 %copy-start = (f32[4096]{0:T(1024)S(1)}, f32[4096]{0:T(1024)}, u32[]{:S(2)}) copy-start(f32[4096]{0:T(1024)} %param.6) | copy-start | bytes 49156
  608.4 53.9 %all-to-all-start = ((bf16[16,256,256]{2,1,0:T(8,128)(2,1)}), bf16[16,256,256]{2,1,0:T(8,128)(2,1)S(1)}, u32[]{:S(2)}, u32[]{:S(2)}) async-start(bf16[16,256,256]{2,1,0:T(8,128)(2,1)} %bitcast.38), calls=%async_computation.2 | async-start | bytes 4194304 | tf_op jit(solution)/shard_map/all_to_all | solution.py:102
Sparse Core Ops, SparseCore 0:
  444.0 18.9 reduce-scatter.2
  465.4 18.0 reduce-scatter.4
where the time goes:
time: 785 us; the launch traced here: 783 us
  other arithmetic  425 us (54%)
  local copies, waits for them, and re-layouts  147 us (19%)
  matrix products  73.4 us (9%)
  waiting for transfers between devices  57.2 us (7%)
  blocking collectives  54.4 us (7%)
  between operations  13.5 us (2%)
  starting transfers between devices  12.7 us (2%)
    reduce_sum x1, other arithmetic, body(): denominator = jnp.sum(weight, axis=0)  343 us
    dynamic_update_slice x16, local copies, waits for them, and re-layouts, cosine_table(): lax.map(lambda first_row: cosine_block(first_row, height, length), starts)  90.8 us
    dot_general x2, matrix products, contract(): lax.dot_general(left, right, (((left_dim,), (right_dim,)), ((), ())), pre...  56.3 us
    all_to_all x1, blocking collectives, body(): lax.all_to_all(back_cols, ('focus', 'strip'), split_axis=0, concat_axis=1...  54.4 us
    all_to_all x1, waiting for transfers between devices, body(): lax.all_to_all(along_cols, ('focus', 'strip'), split_axis=0, concat_axis=...  46.8 us
    slice x1, local copies, waits for them, and re-layouts, body(): center = padded[:, margin:-margin, :]  44.1 us
    convert_element_type x1, other arithmetic, body(): padded = extended(slices, (('strip', 1),), margin).astype(jnp.float32)  32.4 us
    convert_element_type x8, other arithmetic, cosine_block(): return table.reshape(height, length).astype(jnp.bfloat16)  30.1 us
  transfers between devices with their start and end apart: 5, of which 2 were waited for; matrix products, arithmetic and copies ran while one was open for 19% of the time, Pallas kernels for 0%

commit v1 on v0

v1 whole, which is shorter than its diff:
```python
import functools
import math

import jax
import jax.numpy as jnp
import numpy as np
from jax import lax
from jax.experimental import pallas as pl
from jax.experimental.pallas import tpu as pltpu
from jax.sharding import PartitionSpec as P

floor_weight = 0.01
noise_ratio = 0.01
spacings = (1, 2, 4)
margin = 4
edge = 16
lanes = 128
vmem_limit = 56 * 1024 * 1024


def band_matrices(height):
    band = np.zeros((3, height, height), np.float32)
    ends = np.zeros((3, 2, 8, 2 * edge), np.float32)
    for which, d in enumerate(spacings):
        band[which] = np.eye(height, k=d) + np.eye(height, k=-d) - 4.0 * np.eye(height)
        for r in range(d):
            ends[which, 0, r, edge + r - d] = 1.0
            ends[which, 1, 7 - r, edge + d - 1 - r] = 1.0
    return (
        jnp.asarray(band.reshape(3 * height, height), jnp.bfloat16),
        jnp.asarray(ends.reshape(48, 2 * edge), jnp.bfloat16),
    )


def cosine_table(length):
    low_count = 1 << (int(math.log2(length)) // 2)
    high_count = length // low_count
    sample = 2 * np.arange(length, dtype=np.int64) + 1
    unit = math.pi / (2 * length)
    high = (low_count * np.arange(high_count)[:, None] * sample) % (4 * length) * unit
    low = (np.arange(low_count)[:, None] * sample) % (4 * length) * unit
    scale = math.sqrt(2.0 / length)
    high_cos = jnp.asarray(scale * np.cos(high), jnp.float32)[:, None, :]
    high_sin = jnp.asarray(scale * np.sin(high), jnp.float32)[:, None, :]
    low_cos = jnp.asarray(np.cos(low), jnp.float32)[None]
    low_sin = jnp.asarray(np.sin(low), jnp.float32)[None]
    first = np.ones((high_count, low_count, 1), np.float32)
    first[0, 0] = math.sqrt(0.5)
    table = (high_cos * low_cos - high_sin * low_sin) * jnp.asarray(first)
    return table.astype(jnp.bfloat16).reshape(length, length)


def cosine_block(first_row, height, length):
    low_count = min(64, length)
    high_count = length // low_count
    frequency = first_row + lax.broadcasted_iota(jnp.int32, (height, 1), 0)
    high_sample = lax.broadcasted_iota(jnp.int32, (1, high_count), 1)
    low_sample = lax.broadcasted_iota(jnp.int32, (1, low_count), 1)
    high_phase = 2 * low_count * high_sample * frequency % (4 * length)
    low_phase = (2 * low_sample + 1) * frequency % (4 * length)
    unit = jnp.float32(math.pi / (2 * length))
    high_angle = high_phase.astype(jnp.float32) * unit
    low_angle = low_phase.astype(jnp.float32) * unit
    norming = jnp.where(
        frequency == 0, jnp.float32(math.sqrt(1.0 / length)), jnp.float32(math.sqrt(2.0 / length))
    )
    high_cos = (norming * jnp.cos(high_angle))[:, :, None]
    high_sin = (norming * jnp.sin(high_angle))[:, :, None]
    low_cos = jnp.cos(low_angle)[:, None, :]
    low_sin = jnp.sin(low_angle)[:, None, :]
    table = high_cos * low_cos - high_sin * low_sin
    return table.reshape(height, length).astype(jnp.bfloat16)


def cosine_table_plain(length):
    height = min(512, length)
    starts = jnp.arange(length // height, dtype=jnp.int32) * height
    return lax.map(lambda first_row: cosine_block(first_row, height, length), starts).reshape(
        length, length
    )


def stencil_kernel(width, half, main, top, bottom, band, ends, num, den, terms_a, terms_b):
    del half
    height, length = main.shape[1], main.shape[2]
    chunks = length // width

    @pl.when(pl.program_id(0) == 0)
    def _():
        num[...] = jnp.zeros_like(num)
        den[...] = jnp.zeros_like(den)

    def vertical(chunk, terms):
        at = pl.ds(pl.multiple_of(chunk * width, width), width)
        terms[...] = jnp.dot(band[...], main[0, :, at], preferred_element_type=jnp.float32)
        outside = jnp.concatenate([top[0, :, at], bottom[0, :, at]], axis=0)
        extra = jnp.dot(ends[...], outside, preferred_element_type=jnp.float32)
        for which in range(3):
            base = which * height
            terms[base : base + 8, :] += extra[16 * which : 16 * which + 8]
            terms[base + height - 8 : base + height, :] += extra[16 * which + 8 : 16 * which + 16]

    def weigh(chunk, terms):
        start = chunk * width
        at = pl.ds(pl.multiple_of(start, width), width)
        before = pl.ds(pl.multiple_of(jnp.maximum(start - lanes, 0), lanes), lanes)
        after = pl.ds(pl.multiple_of(jnp.minimum(start + width, length - lanes), lanes), lanes)
        has_before = jnp.where(chunk > 0, 1.0, 0.0)
        has_after = jnp.where(chunk < chunks - 1, 1.0, 0.0)
        for row in range(0, height, 16):
            rows = slice(row, row + 16)
            center = main[0, rows, at].astype(jnp.float32)
            wide = jnp.concatenate(
                [
                    main[0, rows, before].astype(jnp.float32) * has_before,
                    center,
                    main[0, rows, after].astype(jnp.float32) * has_after,
                ],
                axis=1,
            )
            full = wide.shape[1]
            lap = []
            for which, d in enumerate(spacings):
                sides = pltpu.roll(wide, d, 1) + pltpu.roll(wide, full - d, 1)
                base = which * height + row
                lap.append(terms[base : base + 16, :] + sides[:, lanes : lanes + width])
            weight = (floor_weight + lap[0] * lap[0]) + 0.5 * (
                lap[1] * lap[1] + 0.5 * (lap[2] * lap[2])
            )
            num[rows, at] += weight * center
            den[rows, at] += weight

    vertical(0, terms_a)

    def pair(index, carry):
        chunk = 2 * index
        vertical(chunk + 1, terms_b)
        weigh(chunk, terms_a)
        vertical(jnp.minimum(chunk + 2, chunks - 1), terms_a)
        weigh(chunk + 1, terms_b)
        return carry

    lax.fori_loop(0, chunks // 2, pair, 0)


def stencil(slices, half, top, bottom, height):
    count, _, length = slices.shape
    width = 256
    band, ends = band_matrices(height)
    sums = jax.ShapeDtypeStruct((height, length), jnp.float32)
    whole = lambda s, h: (0, 0)
    return pl.pallas_call(
        functools.partial(stencil_kernel, width),
        grid_spec=pltpu.PrefetchScalarGridSpec(
            num_scalar_prefetch=1,
            grid=(count,),
            in_specs=[
                pl.BlockSpec((1, height, length), lambda s, h: (s, h[0], 0)),
                pl.BlockSpec((1, edge, length), lambda s, h: (s, 0, 0)),
                pl.BlockSpec((1, edge, length), lambda s, h: (s, 0, 0)),
                pl.BlockSpec(band.shape, whole),
                pl.BlockSpec(ends.shape, whole),
            ],
            out_specs=[pl.BlockSpec((height, length), whole)] * 2,
            scratch_shapes=[pltpu.VMEM((3 * height, width), jnp.float32)] * 2,
        ),
        out_shape=(sums, sums),
        compiler_params=pltpu.CompilerParams(vmem_limit_bytes=vmem_limit),
        cost_estimate=pl.CostEstimate(
            flops=count * height * length * 1600,
            bytes_accessed=count * height * length * 2 + height * length * 8,
            transcendentals=0,
        ),
        name="stencil",
    )(half.reshape(1), slices, top, bottom, band, ends)


def product_cost(rows, length, passes):
    return pl.CostEstimate(
        flops=2 * passes * rows * length * length,
        bytes_accessed=2 * length * length + 8 * rows * length,
        transcendentals=0,
    )


def row_kernel(table, rows, out):
    value = lax.dot_general(
        table[...], rows[...], (((1,), (1,)), ((), ())), preferred_element_type=jnp.float32
    )
    out[...] = value.astype(out.dtype).reshape(out.shape)


def row_transform(cosines, rows, block):
    piece, length = rows.shape
    return pl.pallas_call(
        row_kernel,
        grid=(length // block,),
        in_specs=[
            pl.BlockSpec((block, length), lambda k: (k, 0)),
            pl.BlockSpec((piece, length), lambda k: (0, 0)),
        ],
        out_specs=pl.BlockSpec((block // piece, piece, piece), lambda k: (k, 0, 0)),
        out_shape=jax.ShapeDtypeStruct((length // piece, piece, piece), jnp.bfloat16),
        compiler_params=pltpu.CompilerParams(vmem_limit_bytes=vmem_limit),
        cost_estimate=product_cost(piece, length, 1),
        name="row_transform",
    )(cosines, rows)


def column_kernel(places, table, arrived, rows_otf, cols_otf, out, columns, total):
    piece = arrived.shape[1]
    length = table.shape[1]
    step = pl.program_id(0)

    @pl.when(step == 0)
    def _():
        for source, place in enumerate(places):
            columns[:, place * piece : (place + 1) * piece] = arrived[source]

    spectrum = lax.dot_general(
        table[...], columns[...], (((1,), (1,)), ((), ())), preferred_element_type=jnp.float32
    )
    response = rows_otf[...] * cols_otf[...]
    filtered = spectrum * (response / (response * response + noise_ratio))
    turned = filtered.T.astype(jnp.bfloat16)
    part = 512
    for start in range(0, length, part):
        at = slice(start, start + part)
        value = jnp.dot(turned, table[:, at], preferred_element_type=jnp.float32)

        @pl.when(step == 0)
        def _():
            total[:, at] = value

        @pl.when(step > 0)
        def _():
            total[:, at] += value

    @pl.when(step == pl.num_programs(0) - 1)
    def _():
        for place in range(length // piece):
            out[place] = total[:, place * piece : (place + 1) * piece].astype(out.dtype)


def column_transform(cosines, arrived, rows_otf, cols_otf, places, block):
    count, piece, _ = arrived.shape
    length = count * piece
    whole = lambda u: (0, 0, 0)
    return pl.pallas_call(
        functools.partial(column_kernel, places),
        grid=(length // block,),
        in_specs=[
            pl.BlockSpec((block, length), lambda u: (u, 0)),
            pl.BlockSpec(arrived.shape, whole),
            pl.BlockSpec((block, 1), lambda u: (u, 0)),
            pl.BlockSpec((1, piece), lambda u: (0, 0)),
        ],
        out_specs=pl.BlockSpec((count, piece, piece), whole),
        out_shape=jax.ShapeDtypeStruct((count, piece, piece), jnp.bfloat16),
        scratch_shapes=[
            pltpu.VMEM((piece, length), jnp.bfloat16),
            pltpu.VMEM((piece, length), jnp.float32),
        ],
        compiler_params=pltpu.CompilerParams(vmem_limit_bytes=vmem_limit),
        cost_estimate=product_cost(piece, length, 2),
        name="column_transform",
    )(cosines, arrived, rows_otf[:, None], cols_otf[None, :])


def final_kernel(table, back, out, rows):
    @pl.when(pl.program_id(0) == 0)
    def _():
        count, piece, _ = back.shape
        for source in range(count):
            turned = back[source].astype(jnp.float32).T
            rows[:, source * piece : (source + 1) * piece] = turned.astype(jnp.bfloat16)

    out[...] = jnp.dot(rows[...], table[...], preferred_element_type=jnp.float32)


def final_transform(cosines, back, block):
    count, piece, _ = back.shape
    length = count * piece
    return pl.pallas_call(
        final_kernel,
        grid=(length // block,),
        in_specs=[
            pl.BlockSpec((length, block), lambda n: (0, n)),
            pl.BlockSpec(back.shape, lambda n: (0, 0, 0)),
        ],
        out_specs=pl.BlockSpec((piece, block), lambda n: (0, n)),
        out_shape=jax.ShapeDtypeStruct((piece, length), jnp.float32),
        scratch_shapes=[pltpu.VMEM((piece, length), jnp.bfloat16)],
        compiler_params=pltpu.CompilerParams(vmem_limit_bytes=vmem_limit),
        cost_estimate=product_cost(piece, length, 1),
        name="final_transform",
    )(cosines, back)


def contract(left, right, left_dim, right_dim):
    return lax.dot_general(
        left, right, (((left_dim,), (right_dim,)), ((), ())), preferred_element_type=jnp.float32
    )


def neighbour_rows(slices):
    count = lax.axis_size("strip")
    head = slices[:, :margin]
    tail = slices[:, -margin:]
    above = lax.ppermute(tail, "strip", [(i, i + 1) for i in range(count - 1)])
    below = lax.ppermute(head, "strip", [(i + 1, i) for i in range(count - 1)])
    return above, below


def merged_rows_plain(slices, above, below):
    padded = jnp.concatenate([above, slices, below], axis=1).astype(jnp.float32)
    center = slices.astype(jnp.float32)
    count = center.shape[1]
    weight = floor_weight
    for d, share in zip(spacings, (1.0, 0.5, 0.25)):
        widened = jnp.pad(center, ((0, 0), (0, 0), (d, d)))
        term = padded[:, margin + d : margin + d + count] + padded[:, margin - d : margin - d + count]
        term = term + widened[:, :, 2 * d :] + widened[:, :, : -2 * d] - 4.0 * center
        weight = weight + share * term * term
    numerator = jnp.sum(weight * center, axis=0)
    denominator = jnp.sum(weight, axis=0)
    numerator = lax.psum_scatter(numerator, "focus", scatter_dimension=0, tiled=True)
    denominator = lax.psum_scatter(denominator, "focus", scatter_dimension=0, tiled=True)
    return (numerator / denominator).astype(jnp.bfloat16)


def merged_rows(slices, above, below, piece):
    focus = lax.axis_index("focus")
    rows = slices.shape[1]
    filler = jnp.zeros((slices.shape[0], edge - margin, slices.shape[2]), slices.dtype)
    above = jnp.concatenate([filler, above], axis=1)
    below = jnp.concatenate([below, filler], axis=1)
    inner_above = slices[:, piece - edge : piece]
    inner_below = slices[:, piece : piece + edge]

    def sums(half):
        top = jnp.where(half == 0, above, inner_above)
        bottom = jnp.where(half == 0, inner_below, below)
        return stencil(slices, half, top, bottom, piece)

    swap = [(0, 1), (1, 0)]
    for_partner = sums(1 - focus)
    arrived = [lax.ppermute(part, "focus", swap) for part in for_partner]
    own = sums(focus)
    return ((own[0] + arrived[0]) / (own[1] + arrived[1])).astype(jnp.bfloat16)


def body(slices, otf_rows, otf_cols):
    focus_count = lax.axis_size("focus")
    strip_count = lax.axis_size("strip")
    length = slices.shape[2]
    piece = length // (focus_count * strip_count)
    owners = ("focus", "strip")
    above, below = neighbour_rows(slices)
    owner = lax.axis_index("focus") * strip_count + lax.axis_index("strip")
    local_cols = lax.dynamic_slice_in_dim(otf_cols, owner * piece, piece, 0)
    if piece % lanes == 0 and focus_count == 2 and length % 512 == 0:
        cosines = cosine_table(length)
        block = max(512, piece)
        rows = merged_rows(slices, above, below, piece)
        along_cols = row_transform(cosines, rows, block)
        arrived = lax.all_to_all(along_cols, owners, split_axis=0, concat_axis=0, tiled=True)
        places = [s * focus_count + f for f in range(focus_count) for s in range(strip_count)]
        back = column_transform(cosines, arrived, otf_rows, local_cols, places, block)
        back = lax.all_to_all(back, owners, split_axis=0, concat_axis=0, tiled=True)
        return final_transform(cosines, back, block)
    cosines = cosine_table_plain(length)
    rows = merged_rows_plain(slices, above, below)
    along_cols = contract(cosines, rows, 1, 1).astype(jnp.bfloat16)
    arrived = lax.all_to_all(along_cols, owners, split_axis=0, concat_axis=1, tiled=True)
    column_block = (
        arrived.reshape(piece, focus_count, strip_count, piece)
        .transpose(0, 2, 1, 3)
        .reshape(piece, length)
    )
    spectrum = contract(column_block, cosines, 1, 1)
    response = local_cols[:, None] * otf_rows[None, :]
    filtered = (spectrum * (response / (response * response + noise_ratio))).astype(jnp.bfloat16)
    back_cols = contract(cosines, filtered, 0, 1).astype(jnp.bfloat16)
    rows_back = lax.all_to_all(back_cols, owners, split_axis=0, concat_axis=1, tiled=True)
    return jnp.dot(rows_back, cosines, preferred_element_type=jnp.float32)


def solution(mesh):
    in_specs = (P(("field", "focus"), "strip", None), P(), P())
    out_specs = P(("field", "focus", "strip"), None)
    return jax.shard_map(body, mesh=mesh, in_specs=in_specs, out_specs=out_specs, check_vma=False)
```

time: 785 us -> 412 us (0.52)
  other arithmetic: 425 us -> 69.1 us
  Pallas kernels: 0 us -> 223 us
  local copies, waits for them, and re-layouts: 147 us -> 6.11 us
  matrix products: 73.4 us -> 0 us
  between operations: 13.5 us -> 0.08 us
  waiting for transfers between devices: 57.2 us -> 44.2 us
    reduce_sum x1 -> x0, other arithmetic: 343 us -> none  [body(): denominator = jnp.sum(weight, axis=0)]
    pallas_call x0 -> x5, Pallas kernels: none -> 223 us  [the longest x2 134 us: stencil(): pl.pallas_call(functools.partial(stencil_kernel, width), grid_spec=pltpu....]
    dynamic_update_slice x16 -> x0, local copies, waits for them, and re-layouts: 90.8 us -> none  [cosine_table(): lax.map(lambda first_row: cosine_block(first_row, height, length), starts)]
    dot_general x3 -> x0, matrix products: 73.4 us -> none  [the longest x2 56.3 us: contract(): lax.dot_general(left, right, (((left_dim,), (right_dim,)), ((), ())), pre...]
    slice x2 -> x1, local copies, waits for them, and re-layouts: 45.5 us -> 1.45 us  [neighbour_rows(): head = slices[:, :margin]]
    sub x0 -> x1, other arithmetic: none -> 23.5 us  [cosine_table(): table = (high_cos * low_cos - high_sin * low_sin) * jnp.asarray(first)]
    convert_element_type x9 -> x2, other arithmetic: 62.5 us -> 41.3 us  [the longest x1 32.5 us: cosine_table(): return table.astype(jnp.bfloat16).reshape(length, length)]
    ppermute x2 -> x4, waiting for transfers between devices: 9.85 us -> 0.01 us  [the longest x2 0.01 us: merged_rows(): arrived = [lax.ppermute(part, 'focus', swap) for part in for_partner]]
  transfers between devices with their start and end apart: 5 -> 5, of which waited for: 2 -> 1; matrix products, arithmetic and copies ran while one was open for 19% -> 14% of each run, Pallas kernels for 0% -> 16%
where the time goes in v1:
time: 412 us; the launch traced here: 411 us
  Pallas kernels  223 us (54%)
  other arithmetic  69.1 us (17%)
  blocking collectives  54.7 us (13%)
  waiting for transfers between devices  44.2 us (11%)
  starting transfers between devices  13.8 us (3%)
  local copies, waits for them, and re-layouts  6.11 us (1%)
    pallas_call x2, Pallas kernels, stencil(): pl.pallas_call(functools.partial(stencil_kernel, width), grid_spec=pltpu....  134 us
    all_to_all x1, blocking collectives, body(): back = lax.all_to_all(back, owners, split_axis=0, concat_axis=0, tiled=True)  54.7 us
    pallas_call x1, Pallas kernels, column_transform(): pl.pallas_call(functools.partial(column_kernel, places), grid=(length //...  53.3 us
    all_to_all x1, waiting for transfers between devices, body(): lax.all_to_all(along_cols, owners, split_axis=0, concat_axis=0, tiled=True)  44.2 us
    convert_element_type x1, other arithmetic, cosine_table(): return table.astype(jnp.bfloat16).reshape(length, length)  32.5 us
    sub x1, other arithmetic, cosine_table(): table = (high_cos * low_cos - high_sin * low_sin) * jnp.asarray(first)  23.5 us
    pallas_call x1, Pallas kernels, final_transform(): pl.pallas_call(final_kernel, grid=(length // block,), in_specs=[pl.BlockS...  18.6 us
    pallas_call x1, Pallas kernels, row_transform(): pl.pallas_call(row_kernel, grid=(length // block,), in_specs=[pl.BlockSpe...  17.6 us
  transfers between devices with their start and end apart: 5, of which 1 were waited for; matrix products, arithmetic and copies ran while one was open for 14% of the time, Pallas kernels for 16%

profile of v1, /device:TPU:0, one launch (start us, length us, event | category | flops | bytes accessed | tf_op | source)
XLA Modules:
  0.0 411.5 jit_solution(16451248239005222109)
XLA Ops:
  0.0 1.5 fusion.1
  1.5 1.3 collective-permute-start.1
  2.8 5.5 %collective-permute-start = (bf16[8,4,4096]{2,1,0:T(4,128)(2,1)S(1)}, bf16[8,4,4096]{2,1,0:T(4,128)(2,1)S(1)}, u32[]{:S(2)}, u32[]{:S(2)}) collective-permute-start(bf16[8,4,4096]{2,1,0:T(4,128)(2,1)S(1)} %get-tuple-element.20), channel_id=1, source_target_pairs={{0,1},{1,2},{2,3},{3,4},{4,5},{5,6},{6,7},{8,9},{9,10},{10,11},{11... | collective-permute-start | bytes 786440 | tf_op jit(solution)/shard_map/ppermute | solution.py:310
  8.3 23.5 %multiply_subtract_fusion = f32[64,64,4096]{2,1,0:T(8,128)} fusion(f32[64,4096]{1,0:T(8,128)} %constant.38.clone, f32[64,4096]{1,0:T(8,128)} %constant.36.clone, f32[64,4096]{1,0:T(8,128)} %constant.37.clone, f32[64,4096]{1,0:T(8,128)} %constant.35.clone), kind=kLoop, calls=%fused_computation.2 | loop fusion | flops 50331648 | bytes 71303168 | tf_op jit(solution)/shard_map/sub | solution.py:49
  31.8 0.0 collective-permute-done.1
  31.9 0.0 collective-permute-done
  31.9 4.3 %pad_select_fusion = (bf16[8,16,4096]{2,1,0:T(8,128)(2,1)}, bf16[8,16,4096]{2,1,0:T(8,128)(2,1)}, bf16[8,16,4096]{2,1,0:T(8,128)(2,1)}, bf16[8,16,4096]{2,1,0:T(8,128)(2,1)}) fusion(bf16[8,4,4096]{2,1,0:T(4,128)(2,1)S(1)} %collective-permute-done.1, pred[]{:T(512)S(6)} %eq.9, bf16[8,512,4096]{2,1,0:T(8,128)(2,1)} %main.3, pred[]{:T(512)S(6)} %eq.8, ...), kind=kLoop, calls=%fused_computation.4 | loop fusion | flops 2097152 | bytes 6815746 | tf_op jit(solution)/shard_map/jit(_where)/select_n | solution.py:343
  36.1 67.0 %stencil.3 = (f32[256,4096]{1,0:T(8,128)}, f32[256,4096]{1,0:T(8,128)}) custom-call(s32[1]{0:T(128)} %bitcast.2.half, bf16[8,512,4096]{2,1,0:T(8,128)(2,1)} %main.3, bf16[8,16,4096]{2,1,0:T(8,128)(2,1)} %get-tuple-element.18.top, bf16[8,16,4096]{2,1,0:T(8,128)(2,1)} %get-tuple-element.13.bottom, bf16[768,256]{1,0:T(8,128)(2,1)} %constant.40.clone.band, ...), custom_call_target="tpu_custom_call" | custom-call | flops 13421772800 | bytes 25165824 | tf_op jit(solution)/shard_map/stencil/pallas_call | solution.py:152
  103.2 0.0 collective-permute-start.3
  103.2 0.5 collective-permute-start.2
  103.7 32.5 %fusion.table = bf16[4096,4096]{1,0:T(8,128)(2,1)} fusion(f32[64,64,4096]{2,1,0:T(8,128)} %multiply_subtract_fusion, f32[4096]{0:T(1024)S(1)} %copy-done.2), kind=kLoop, calls=%fused_computation.1 | loop fusion | flops 33554432 | bytes 100679680 | tf_op jit(solution)/shard_map/convert_element_type | solution.py:50
  136.2 67.1 %stencil.2 = (f32[256,4096]{1,0:T(8,128)}, f32[256,4096]{1,0:T(8,128)}) custom-call(s32[1]{0:T(128)} %bitcast.1.half, bf16[8,512,4096]{2,1,0:T(8,128)(2,1)} %main.3, bf16[8,16,4096]{2,1,0:T(8,128)(2,1)} %get-tuple-element.17.top, bf16[8,16,4096]{2,1,0:T(8,128)(2,1)} %get-tuple-element.14.bottom, bf16[768,256]{1,0:T(8,128)(2,1)} %constant.40.clone.band, ...), custom_call_target="tpu_custom_call" | custom-call | flops 13421772800 | bytes 25165824 | tf_op jit(solution)/shard_map/stencil/pallas_call | solution.py:152
  203.3 0.0 collective-permute-done.3
  203.3 0.0 collective-permute-done.2
  203.3 8.8 %divide_convert_fusion.rows = bf16[256,4096]{1,0:T(8,128)(2,1)} fusion(f32[256,4096]{1,0:T(8,128)} %get-tuple-element.11, f32[256,4096]{1,0:T(8,128)} %collective-permute-done.3, f32[256,4096]{1,0:T(8,128)} %get-tuple-element.9, f32[256,4096]{1,0:T(8,128)} %collective-permute-done.2), kind=kLoop, calls=%fused_computation.3 | loop fusion | flops 4194304 | bytes 18874368 | tf_op jit(solution)/shard_map/convert_element_type | solution.py:350
  212.0 17.6 %row_transform.1 = bf16[16,256,256]{2,1,0:T(8,128)(2,1)} custom-call(bf16[4096,4096]{1,0:T(8,128)(2,1)} %fusion.table, bf16[256,4096]{1,0:T(8,128)(2,1)} %divide_convert_fusion.rows), custom_call_target="tpu_custom_call" | custom-call | flops 8589934592 | bytes 41943040 | tf_op jit(solution)/shard_map/row_transform/pallas_call | solution.py:195
  229.6 6.4 %all-to-all-start = ((bf16[16,256,256]{2,1,0:T(8,128)(2,1)}), bf16[16,256,256]{2,1,0:T(8,128)(2,1)S(1)}, u32[]{:S(2)}, u32[]{:S(2)}) async-start(bf16[16,256,256]{2,1,0:T(8,128)(2,1)} %row_transform.1), calls=%async_computation | async-start | bytes 4194304 | tf_op jit(solution)/shard_map/all_to_all | solution.py:367
  236.1 2.0 copy.13.rows_otf
  238.0 1.4 dynamic_slice.3
  239.4 44.2 %all-to-all-done.arrived = bf16[16,256,256]{2,1,0:T(8,128)(2,1)S(1)} async-done(((bf16[16,256,256]{2,1,0:T(8,128)(2,1)}), bf16[16,256,256]{2,1,0:T(8,128)(2,1)S(1)}, u32[]{:S(2)}, u32[]{:S(2)}) %all-to-all-start) | async-done | bytes 2097184 | tf_op jit(solution)/shard_map/all_to_all | solution.py:367
  283.6 1.3 copy-done
  284.9 53.3 %column_transform.1 = bf16[16,256,256]{2,1,0:T(8,128)(2,1)} custom-call(bf16[4096,4096]{1,0:T(8,128)(2,1)} %fusion.table, bf16[16,256,256]{2,1,0:T(8,128)(2,1)} %copy-done, f32[4096,1]{1,0:T(8,128)} %copy.13.rows_otf, f32[1,256]{1,0:T(1,128)} %bitcast.9), custom_call_target="tpu_custom_call" | custom-call | flops 17179869184 | bytes 41943040 | tf_op jit(solution)/shard_map/column_transform/pallas_call | solution.py:249
  338.2 54.7 %all_to_all.10.back = bf16[16,256,256]{2,1,0:T(8,128)(2,1)} all-to-all(bf16[16,256,256]{2,1,0:T(8,128)(2,1)} %column_transform.1), channel_id=1, replica_groups=mesh['field'=2,'focus'=2,'strip'=8] {'focus','strip'}, dimensions={0} | all-to-all | bytes 4194304 | tf_op jit(solution)/shard_map/all_to_all | solution.py:370
  392.9 18.6 %final_transform.1 = f32[256,4096]{1,0:T(8,128)} custom-call(bf16[4096,4096]{1,0:T(8,128)(2,1)} %fusion.table, bf16[16,256,256]{2,1,0:T(8,128)(2,1)} %all_to_all.10.back), custom_call_target="tpu_custom_call" | custom-call | flops 8589934592 | bytes 41943040 | tf_op jit(solution)/shard_map/final_transform/pallas_call | solution.py:284
  (5 shorter events, 0.0 us)
Async XLA Ops:
  1.5 30.4 %collective-permute-start.1 = (bf16[8,4,4096]{2,1,0:T(4,128)(2,1)S(1)}, bf16[8,4,4096]{2,1,0:T(4,128)(2,1)S(1)}, u32[]{:S(2)}, u32[]{:S(2)}) collective-permute-start(bf16[8,4,4096]{2,1,0:T(4,128)(2,1)S(1)} %get-tuple-element.19), channel_id=1, source_target_pairs={{1,0},{2,1},{3,2},{4,3},{5,4},{6,5},{7,6},{9,8},{10,9},{11,10},{12... | collective-permute-start | bytes 786440 | tf_op jit(solution)/shard_map/ppermute | solution.py:311
  2.8 29.1 %collective-permute-start = (bf16[8,4,4096]{2,1,0:T(4,128)(2,1)S(1)}, bf16[8,4,4096]{2,1,0:T(4,128)(2,1)S(1)}, u32[]{:S(2)}, u32[]{:S(2)}) collective-permute-start(bf16[8,4,4096]{2,1,0:T(4,128)(2,1)S(1)} %get-tuple-element.20), channel_id=1, source_target_pairs={{0,1},{1,2},{2,3},{3,4},{4,5},{5,6},{6,7},{8,9},{9,10},{10,11},{11... | collective-permute-start | bytes 786440 | tf_op jit(solution)/shard_map/ppermute | solution.py:310
  36.1 67.6 %copy-start.2 = (f32[4096]{0:T(1024)S(1)}, f32[4096]{0:T(1024)}, u32[]{:S(2)}) copy-start(f32[4096]{0:T(1024)} %constant.46) | copy-start | bytes 49156
  103.2 100.1 %collective-permute-start.3 = (f32[256,4096]{1,0:T(8,128)}, f32[256,4096]{1,0:T(8,128)}, u32[]{:S(2)}, u32[]{:S(2)}) collective-permute-start(f32[256,4096]{1,0:T(8,128)} %get-tuple-element.12), channel_id=1, source_target_pairs={{0,8},{8,0},{1,9},{9,1},{2,10},{10,2},{3,11},{11,3},{4,12},{12,4},... | collective-permute-start | bytes 12582920 | tf_op jit(solution)/shard_map/ppermute | solution.py:348
  103.2 100.1 %collective-permute-start.2 = (f32[256,4096]{1,0:T(8,128)}, f32[256,4096]{1,0:T(8,128)}, u32[]{:S(2)}, u32[]{:S(2)}) collective-permute-start(f32[256,4096]{1,0:T(8,128)} %get-tuple-element.10), channel_id=1, source_target_pairs={{0,8},{8,0},{1,9},{9,1},{2,10},{10,2},{3,11},{11,3},{4,12},{12,4},... | collective-permute-start | bytes 12582920 | tf_op jit(solution)/shard_map/ppermute | solution.py:348
  229.6 6.5 %copy-start.1 = (f32[4096]{0:T(1024)S(1)}, f32[4096]{0:T(1024)}, u32[]{:S(2)}) copy-start(f32[4096]{0:T(1024)} %param.13) | copy-start | bytes 49156
  229.6 54.0 %all-to-all-start = ((bf16[16,256,256]{2,1,0:T(8,128)(2,1)}), bf16[16,256,256]{2,1,0:T(8,128)(2,1)S(1)}, u32[]{:S(2)}, u32[]{:S(2)}) async-start(bf16[16,256,256]{2,1,0:T(8,128)(2,1)} %row_transform.1), calls=%async_computation | async-start | bytes 4194304 | tf_op jit(solution)/shard_map/all_to_all | solution.py:367
  283.6 1.3 copy-start

commit v2 on v1

--- a/solution.py
+++ b/solution.py
@@ -32,6 +32,17 @@
     )
 
 
+def table_kernel(high_cos, high_sin, low_cos, low_sin, out):
+    value = high_cos[0] * low_cos[...] - high_sin[0] * low_sin[...]
+    out[...] = value.astype(out.dtype)
+
+    @pl.when(pl.program_id(0) == 0)
+    def _():
+        top = high_cos[0] * low_cos[:16, :] - high_sin[0] * low_sin[:16, :]
+        row = lax.broadcasted_iota(jnp.int32, top.shape, 0)
+        out[:16, :] = jnp.where(row == 0, top * math.sqrt(0.5), top).astype(out.dtype)
+
+
 def cosine_table(length):
     low_count = 1 << (int(math.log2(length)) // 2)
     high_count = length // low_count
@@ -42,12 +53,22 @@
     scale = math.sqrt(2.0 / length)
     high_cos = jnp.asarray(scale * np.cos(high), jnp.float32)[:, None, :]
     high_sin = jnp.asarray(scale * np.sin(high), jnp.float32)[:, None, :]
-    low_cos = jnp.asarray(np.cos(low), jnp.float32)[None]
-    low_sin = jnp.asarray(np.sin(low), jnp.float32)[None]
-    first = np.ones((high_count, low_count, 1), np.float32)
-    first[0, 0] = math.sqrt(0.5)
-    table = (high_cos * low_cos - high_sin * low_sin) * jnp.asarray(first)
-    return table.astype(jnp.bfloat16).reshape(length, length)
+    low_cos = jnp.asarray(np.cos(low), jnp.float32)
+    low_sin = jnp.asarray(np.sin(low), jnp.float32)
+    high_block = pl.BlockSpec((1, 1, length), lambda k: (k, 0, 0))
+    low_block = pl.BlockSpec((low_count, length), lambda k: (0, 0))
+    return pl.pallas_call(
+        table_kernel,
+        grid=(high_count,),
+        in_specs=[high_block, high_block, low_block, low_block],
+        out_specs=pl.BlockSpec((low_count, length), lambda k: (k, 0)),
+        out_shape=jax.ShapeDtypeStruct((length, length), jnp.bfloat16),
+        compiler_params=pltpu.CompilerParams(vmem_limit_bytes=vmem_limit),
+        cost_estimate=pl.CostEstimate(
+            flops=3 * length * length, bytes_accessed=2 * length * length, transcendentals=0
+        ),
+        name="cosine_table",
+    )(high_cos, high_sin, low_cos, low_sin)
 
 
 def cosine_block(first_row, height, length):
@@ -145,7 +166,7 @@
 
 def stencil(slices, half, top, bottom, height):
     count, _, length = slices.shape
-    width = 256
+    width = 512
     band, ends = band_matrices(height)
     sums = jax.ShapeDtypeStruct((height, length), jnp.float32)
     whole = lambda s, h: (0, 0)
@@ -359,14 +380,14 @@
     above, below = neighbour_rows(slices)
     owner = lax.axis_index("focus") * strip_count + lax.axis_index("strip")
     local_cols = lax.dynamic_slice_in_dim(otf_cols, owner * piece, piece, 0)
-    if piece % lanes == 0 and focus_count == 2 and length % 512 == 0:
+    if piece % lanes == 0 and focus_count == 2 and length % 1024 == 0:
         cosines = cosine_table(length)
         block = max(512, piece)
         rows = merged_rows(slices, above, below, piece)
         along_cols = row_transform(cosines, rows, block)
         arrived = lax.all_to_all(along_cols, owners, split_axis=0, concat_axis=0, tiled=True)
         places = [s * focus_count + f for f in range(focus_count) for s in range(strip_count)]
-        back = column_transform(cosines, arrived, otf_rows, local_cols, places, block)
+        back = column_transform(cosines, arrived, otf_rows, local_cols, places, 2 * block)
         back = lax.all_to_all(back, owners, split_axis=0, concat_axis=0, tiled=True)
         return final_transform(cosines, back, block)
     cosines = cosine_table_plain(length)

time: 412 us -> 376 us (0.913)
  other arithmetic: 69.1 us -> 11.8 us
  waiting for transfers between devices: 44.2 us -> 54 us
  Pallas kernels: 223 us -> 232 us
    pallas_call x0 -> x1, Pallas kernels: none -> 38.3 us  [cosine_table(): pl.pallas_call(table_kernel, grid=(high_count,), in_specs=[high_block, hi...]
    convert_element_type x1 -> x0, other arithmetic: 32.5 us -> none  [cosine_table(): return table.astype(jnp.bfloat16).reshape(length, length)]
    pallas_call x2, Pallas kernels: 134 us -> 110 us  [stencil(): pl.pallas_call(functools.partial(stencil_kernel, width), grid_spec=pltpu....]
    sub x1 -> x0, other arithmetic: 23.5 us -> none  [cosine_table(): table = (high_cos * low_cos - high_sin * low_sin) * jnp.asarray(first)]
    ppermute x1, waiting for transfers between devices: 0.01 us -> 9.84 us  [neighbour_rows(): above = lax.ppermute(tail, 'strip', [(i, i + 1) for i in range(count - 1)])]
    pallas_call x1, Pallas kernels: 53.3 us -> 46.8 us  [column_transform(): pl.pallas_call(functools.partial(column_kernel, places), grid=(length //...]
  transfers between devices with their start and end apart: 5 -> 5, of which waited for: 1 -> 2; matrix products, arithmetic and copies ran while one was open for 14% -> 1% of each run, Pallas kernels for 16% -> 25%
where the time goes in v2:
time: 376 us; the launch traced here: 372 us
  Pallas kernels  232 us (62%)
  blocking collectives  54.7 us (15%)
  waiting for transfers between devices  54 us (14%)
  starting transfers between devices  13.7 us (4%)
  other arithmetic  11.8 us (3%)
  local copies, waits for them, and re-layouts  6.13 us (2%)
    pallas_call x2, Pallas kernels, stencil(): pl.pallas_call(functools.partial(stencil_kernel, width), grid_spec=pltpu....  110 us
    all_to_all x1, blocking collectives, body(): back = lax.all_to_all(back, owners, split_axis=0, concat_axis=0, tiled=True)  54.7 us
    pallas_call x1, Pallas kernels, column_transform(): pl.pallas_call(functools.partial(column_kernel, places), grid=(length //...  46.8 us
    all_to_all x1, waiting for transfers between devices, body(): lax.all_to_all(along_cols, owners, split_axis=0, concat_axis=0, tiled=True)  44.2 us
    pallas_call x1, Pallas kernels, cosine_table(): pl.pallas_call(table_kernel, grid=(high_count,), in_specs=[high_block, hi...  38.3 us
    pallas_call x1, Pallas kernels, final_transform(): pl.pallas_call(final_kernel, grid=(length // block,), in_specs=[pl.BlockS...  18.6 us
    pallas_call x1, Pallas kernels, row_transform(): pl.pallas_call(row_kernel, grid=(length // block,), in_specs=[pl.BlockSpe...  17.6 us
    ppermute x1, waiting for transfers between devices, neighbour_rows(): above = lax.ppermute(tail, 'strip', [(i, i + 1) for i in range(count - 1)])  9.84 us
  transfers between devices with their start and end apart: 5, of which 2 were waited for; matrix products, arithmetic and copies ran while one was open for 1% of the time, Pallas kernels for 25%

profile of v2, /device:TPU:0, one launch (start us, length us, event | category | flops | bytes accessed | tf_op | source)
XLA Modules:
  0.0 372.1 jit_solution(14753855963314166159)
XLA Ops:
  0.0 1.5 fusion
  1.5 4.9 %collective-permute-start = (bf16[8,4,4096]{2,1,0:T(4,128)(2,1)S(1)}, bf16[8,4,4096]{2,1,0:T(4,128)(2,1)S(1)}, u32[]{:S(2)}, u32[]{:S(2)}) collective-permute-start(bf16[8,4,4096]{2,1,0:T(4,128)(2,1)S(1)} %get-tuple-element.20), channel_id=1, source_target_pairs={{0,1},{1,2},{2,3},{3,4},{4,5},{5,6},{6,7},{8,9},{9,10},{10,11},{11... | collective-permute-start | bytes 786440 | tf_op jit(solution)/shard_map/ppermute | solution.py:331
  6.4 1.3 collective-permute-start.1
  7.7 9.8 %collective-permute-done = bf16[8,4,4096]{2,1,0:T(4,128)(2,1)S(1)} collective-permute-done((bf16[8,4,4096]{2,1,0:T(4,128)(2,1)S(1)}, bf16[8,4,4096]{2,1,0:T(4,128)(2,1)S(1)}, u32[]{:S(2)}, u32[]{:S(2)}) %collective-permute-start) | collective-permute-done | bytes 262176 | tf_op jit(solution)/shard_map/ppermute | solution.py:331
  17.5 0.0 collective-permute-done.1
  17.5 4.2 %pad_select_fusion = (bf16[8,16,4096]{2,1,0:T(8,128)(2,1)}, bf16[8,16,4096]{2,1,0:T(8,128)(2,1)}, bf16[8,16,4096]{2,1,0:T(8,128)(2,1)}, bf16[8,16,4096]{2,1,0:T(8,128)(2,1)}) fusion(bf16[8,4,4096]{2,1,0:T(4,128)(2,1)S(1)} %collective-permute-done.1, pred[]{:T(512)S(6)} %eq.9, bf16[8,512,4096]{2,1,0:T(8,128)(2,1)} %main.3, pred[]{:T(512)S(6)} %eq.8, ...), kind=kLoop, calls=%fused_computation.1 | loop fusion | flops 2097152 | bytes 6815746 | tf_op jit(solution)/shard_map/jit(_where)/select_n | solution.py:364
  21.7 55.2 %stencil.3 = (f32[256,4096]{1,0:T(8,128)}, f32[256,4096]{1,0:T(8,128)}) custom-call(s32[1]{0:T(128)} %bitcast.1.half, bf16[8,512,4096]{2,1,0:T(8,128)(2,1)} %main.3, bf16[8,16,4096]{2,1,0:T(8,128)(2,1)} %get-tuple-element.18.top, bf16[8,16,4096]{2,1,0:T(8,128)(2,1)} %get-tuple-element.13.bottom, bf16[768,256]{1,0:T(8,128)(2,1)} %constant.37.clone.band, ...), custom_call_target="tpu_custom_call" | custom-call | flops 13421772800 | bytes 25165824 | tf_op jit(solution)/shard_map/stencil/pallas_call | solution.py:173
  76.9 0.0 collective-permute-start.2
  76.9 0.5 collective-permute-start.3
  77.4 38.3 %cosine_table.1.table = bf16[4096,4096]{1,0:T(8,128)(2,1)} custom-call(f32[64,1,4096]{2,1,0:T(1,128)} %constant.43.high_cos, f32[64,1,4096]{2,1,0:T(1,128)} %constant.44.high_sin, f32[64,4096]{1,0:T(8,128)} %constant.35.clone.low_cos, f32[64,4096]{1,0:T(8,128)} %constant.36.clone.low_sin), custom_call_target="tpu_custom_call" | custom-call | flops 50331648 | bytes 33554432 | tf_op jit(solution)/shard_map/cosine_table/pallas_call | solution.py:60
  115.7 55.3 %stencil.2 = (f32[256,4096]{1,0:T(8,128)}, f32[256,4096]{1,0:T(8,128)}) custom-call(s32[1]{0:T(128)} %bitcast.half, bf16[8,512,4096]{2,1,0:T(8,128)(2,1)} %main.3, bf16[8,16,4096]{2,1,0:T(8,128)(2,1)} %get-tuple-element.17.top, bf16[8,16,4096]{2,1,0:T(8,128)(2,1)} %get-tuple-element.14.bottom, bf16[768,256]{1,0:T(8,128)(2,1)} %constant.37.clone.band, ...), custom_call_target="tpu_custom_call" | custom-call | flops 13421772800 | bytes 25165824 | tf_op jit(solution)/shard_map/stencil/pallas_call | solution.py:173
  171.0 0.0 collective-permute-done.2
  171.0 0.0 collective-permute-done.3
  171.0 7.6 %divide_convert_fusion.rows = bf16[256,4096]{1,0:T(8,128)(2,1)} fusion(f32[256,4096]{1,0:T(8,128)} %get-tuple-element.11, f32[256,4096]{1,0:T(8,128)} %collective-permute-done.3, f32[256,4096]{1,0:T(8,128)} %get-tuple-element.9, f32[256,4096]{1,0:T(8,128)S(1)} %collective-permute-done.2), kind=kLoop, calls=%fused_computation | loop fusion | flops 4194304 | bytes 18874368 | tf_op jit(solution)/shard_map/convert_element_type | solution.py:371
  178.6 17.6 %row_transform.1 = bf16[16,256,256]{2,1,0:T(8,128)(2,1)} custom-call(bf16[4096,4096]{1,0:T(8,128)(2,1)} %cosine_table.1.table, bf16[256,4096]{1,0:T(8,128)(2,1)} %divide_convert_fusion.rows), custom_call_target="tpu_custom_call" | custom-call | flops 8589934592 | bytes 41943040 | tf_op jit(solution)/shard_map/row_transform/pallas_call | solution.py:216
  196.2 7.0 %all-to-all-start = ((bf16[16,256,256]{2,1,0:T(8,128)(2,1)}), bf16[16,256,256]{2,1,0:T(8,128)(2,1)S(1)}, u32[]{:S(2)}, u32[]{:S(2)}) async-start(bf16[16,256,256]{2,1,0:T(8,128)(2,1)} %row_transform.1), calls=%async_computation | async-start | bytes 4194304 | tf_op jit(solution)/shard_map/all_to_all | solution.py:388
  203.1 0.0 copy-done.1
  203.1 2.0 copy.12.rows_otf
  205.2 1.3 dynamic_slice.3
  206.5 44.2 %all-to-all-done.arrived = bf16[16,256,256]{2,1,0:T(8,128)(2,1)S(1)} async-done(((bf16[16,256,256]{2,1,0:T(8,128)(2,1)}), bf16[16,256,256]{2,1,0:T(8,128)(2,1)S(1)}, u32[]{:S(2)}, u32[]{:S(2)}) %all-to-all-start) | async-done | bytes 2097184 | tf_op jit(solution)/shard_map/all_to_all | solution.py:388
  250.7 1.3 copy-done
  252.0 46.8 %column_transform.1 = bf16[16,256,256]{2,1,0:T(8,128)(2,1)} custom-call(bf16[4096,4096]{1,0:T(8,128)(2,1)} %cosine_table.1.table, bf16[16,256,256]{2,1,0:T(8,128)(2,1)} %copy-done, f32[4096,1]{1,0:T(8,128)} %copy.12.rows_otf, f32[1,256]{1,0:T(1,128)} %bitcast.5), custom_call_target="tpu_custom_call" | custom-call | flops 17179869184 | bytes 41943040 | tf_op jit(solution)/shard_map/column_transform/pallas_call | solution.py:270
  298.8 54.7 %all_to_all.10.back = bf16[16,256,256]{2,1,0:T(8,128)(2,1)} all-to-all(bf16[16,256,256]{2,1,0:T(8,128)(2,1)} %column_transform.1), channel_id=1, replica_groups=mesh['field'=2,'focus'=2,'strip'=8] {'focus','strip'}, dimensions={0} | all-to-all | bytes 4194304 | tf_op jit(solution)/shard_map/all_to_all | solution.py:391
  353.5 18.6 %final_transform.1 = f32[256,4096]{1,0:T(8,128)} custom-call(bf16[4096,4096]{1,0:T(8,128)(2,1)} %cosine_table.1.table, bf16[16,256,256]{2,1,0:T(8,128)(2,1)} %all_to_all.10.back), custom_call_target="tpu_custom_call" | custom-call | flops 8589934592 | bytes 41943040 | tf_op jit(solution)/shard_map/final_transform/pallas_call | solution.py:305
  (2 shorter events, 0.0 us)
Async XLA Ops:
  1.5 16.0 %collective-permute-start = (bf16[8,4,4096]{2,1,0:T(4,128)(2,1)S(1)}, bf16[8,4,4096]{2,1,0:T(4,128)(2,1)S(1)}, u32[]{:S(2)}, u32[]{:S(2)}) collective-permute-start(bf16[8,4,4096]{2,1,0:T(4,128)(2,1)S(1)} %get-tuple-element.20), channel_id=1, source_target_pairs={{0,1},{1,2},{2,3},{3,4},{4,5},{5,6},{6,7},{8,9},{9,10},{10,11},{11... | collective-permute-start | bytes 786440 | tf_op jit(solution)/shard_map/ppermute | solution.py:331
  6.4 11.2 %collective-permute-start.1 = (bf16[8,4,4096]{2,1,0:T(4,128)(2,1)S(1)}, bf16[8,4,4096]{2,1,0:T(4,128)(2,1)S(1)}, u32[]{:S(2)}, u32[]{:S(2)}) collective-permute-start(bf16[8,4,4096]{2,1,0:T(4,128)(2,1)S(1)} %get-tuple-element.19), channel_id=1, source_target_pairs={{1,0},{2,1},{3,2},{4,3},{5,4},{6,5},{7,6},{9,8},{10,9},{11,10},{12... | collective-permute-start | bytes 786440 | tf_op jit(solution)/shard_map/ppermute | solution.py:332
  76.9 94.1 %collective-permute-start.2 = (f32[256,4096]{1,0:T(8,128)}, f32[256,4096]{1,0:T(8,128)S(1)}, u32[]{:S(2)}, u32[]{:S(2)}) collective-permute-start(f32[256,4096]{1,0:T(8,128)} %get-tuple-element.10), channel_id=1, source_target_pairs={{0,8},{8,0},{1,9},{9,1},{2,10},{10,2},{3,11},{11,3},{4,12},{12,4},... | collective-permute-start | bytes 12582920 | tf_op jit(solution)/shard_map/ppermute | solution.py:369
  76.9 94.1 %collective-permute-start.3 = (f32[256,4096]{1,0:T(8,128)}, f32[256,4096]{1,0:T(8,128)}, u32[]{:S(2)}, u32[]{:S(2)}) collective-permute-start(f32[256,4096]{1,0:T(8,128)} %get-tuple-element.12), channel_id=1, source_target_pairs={{0,8},{8,0},{1,9},{9,1},{2,10},{10,2},{3,11},{11,3},{4,12},{12,4},... | collective-permute-start | bytes 12582920 | tf_op jit(solution)/shard_map/ppermute | solution.py:369
  196.1 7.0 %copy-start.1 = (f32[4096]{0:T(1024)S(1)}, f32[4096]{0:T(1024)}, u32[]{:S(2)}) copy-start(f32[4096]{0:T(1024)} %param.12) | copy-start | bytes 49156
  196.2 54.5 %all-to-all-start = ((bf16[16,256,256]{2,1,0:T(8,128)(2,1)}), bf16[16,256,256]{2,1,0:T(8,128)(2,1)S(1)}, u32[]{:S(2)}, u32[]{:S(2)}) async-start(bf16[16,256,256]{2,1,0:T(8,128)(2,1)} %row_transform.1), calls=%async_computation | async-start | bytes 4194304 | tf_op jit(solution)/shard_map/all_to_all | solution.py:388
  250.7 1.3 copy-start
